TPU v7x, 32 devices: a whole 2x2x4 slice. The times are simulated.
32 devices in a mesh: parts: 2 (over y), seq: 4 (over x, core), tensor: 4 (over z).
Axes of the slice: x: 2, y: 2, z: 4, core: 2. Of those that a mesh axis runs over, the one named last changes fastest.
Arguments:
- token_ids: int32 [2048], P(('parts', 'seq')), parts along dimension 0, may hold values from 0 to 511
- embed: bfloat16 [512, 8192], P(None, 'tensor'), may hold values from -6 to 6
- norm_gain_vector: float32 [8192], P('tensor'), may hold values from 0.25 to 1.75
- base_proj: bfloat16 [3, 2048, 8192], P(None, ('parts', 'seq'), 'tensor'), parts along dimension 1, may hold values from -6 to 6
- adapter_down_matrices: bfloat16 [8192, 384], P('tensor'), may hold values from -0.0625 to 0.0625
- adapter_up_matrices: bfloat16 [3, 128, 8192], P(None, None, 'tensor'), may hold values from -0.5 to 0.5
- short_taps: float32 [3, 7, 8192], P(None, None, 'tensor'), may hold values from -2 to 2
- medium_taps: float32 [128, 8192], P(None, 'tensor'), may hold values from -0.5 to 0.5
- skip_gain: float32 [8192], P('tensor'), may hold values from 0.25 to 1.75
- mixer_cot: bfloat16 [2048, 8192], P(('parts', 'seq'), 'tensor'), parts along dimension 0, may hold values from -6 to 6
- bucket_ids: int32 [8192], P('tensor'), may hold values from 0 to 31
Outputs:
- features: float32 [4, 16, 384], P('parts'), parts along dimension 0
There are 2 independent parts, one for each index of `parts`. A program takes and returns all parts, laid end to end along the dimension named above; an argument that names none is the same for every part. Nothing has to cross between parts.
All inputs are finite; a program needn't handle non-finite values.
Results may differ from a plain program's by a relative error of at most 0.0069.
Values sent between devices are 32-bit elements; how exact they have to be, the bound alone decides.
A program may use at most 192 MiB of HBM per device.

v0:
```python
import jax
import jax.numpy as jnp
import numpy as np
from jax import lax
from jax.sharding import PartitionSpec as P

BUCKETS = 16
NORM_EPS = 1e-05
FEATURE_EPS = 1e-06
ADAPTER_SCALE = 1.5
RIM = 8
BF = jnp.bfloat16
F32 = jnp.float32


def from_behind(array, axis, by):
    count = lax.axis_size(axis)
    pairs = [(i, i + by) for i in range(count) if 0 <= i + by < count]
    return lax.ppermute(array, axis, pairs)


def spectrum_tables(rows, span):
    ext = rows + RIM + span
    half = -(-ext // 32) * 16
    period = 2 * half
    omega = 2.0 * np.pi * (np.arange(half) + 0.5) / period
    angle = omega[:, None] * np.arange(ext)[None, :]
    fwd = np.concatenate([np.cos(angle), -np.sin(angle)], axis=0)
    inv = fwd.T * (4.0 / period)
    return (fwd, inv)


def on_device(
    token_ids,
    embed,
    norm_gain_vector,
    base_proj,
    adapter_down_matrices,
    adapter_up_matrices,
    short_taps,
    medium_taps,
    skip_gain,
    mixer_cot,
    bucket_ids,
):
    rows = token_ids.shape[0]
    vocab = embed.shape[0]
    width = embed.shape[1]
    rank = adapter_up_matrices.shape[1]
    span = medium_taps.shape[0]
    taps = short_taps.shape[1]
    full = width * lax.axis_size("tensor")
    out_rows = rows + RIM
    ids = token_ids + 1
    ids_ext = jnp.concatenate(
        [from_behind(ids[rows - RIM :], "seq", 1), ids, from_behind(ids[:RIM], "seq", -1)]
    )
    base_ext = jnp.concatenate(
        [
            from_behind(base_proj[:, rows - RIM :].astype(F32), "seq", 1),
            base_proj.astype(F32),
            from_behind(base_proj[:, :RIM].astype(F32), "seq", -1),
        ],
        axis=1,
    )
    cot = mixer_cot.astype(F32)
    cot_ext = jnp.concatenate([cot, from_behind(cot[:RIM], "seq", -1)], axis=0)
    sketch = jnp.where(bucket_ids >= BUCKETS, -1.0, 1.0)[:, None] * (
        (bucket_ids % BUCKETS)[:, None] == jnp.arange(BUCKETS, dtype=jnp.int32)[None, :]
    )
    sketch = sketch.astype(BF)
    one_hot = (ids_ext[:, None] == 1 + jnp.arange(vocab, dtype=jnp.int32)[None, :]).astype(BF)
    inputs = jnp.dot(one_hot, embed, preferred_element_type=F32)
    squares = jnp.sum(inputs * inputs, axis=1, keepdims=True)
    gained = (inputs * norm_gain_vector).astype(BF)
    down = jnp.concatenate([adapter_down_matrices, sketch], axis=1)
    piece = jnp.dot(gained, down, preferred_element_type=F32)
    total = lax.psum(jnp.concatenate([piece, squares], axis=1), "tensor")
    scale = lax.rsqrt(total[:, -1:] / full + NORM_EPS)
    low = (total[:, : 3 * rank] * (scale * ADAPTER_SCALE)).astype(BF)
    token_sketch = (total[:, 3 * rank : -1] * scale)[RIM : RIM + rows]
    pre_mix = base_ext + jnp.einsum(
        "tsr,src->stc", low.reshape(-1, 3, rank), adapter_up_matrices, preferred_element_type=F32
    )
    filtered = sum(
        (
            short_taps[:, j][:, None, :] * pre_mix[:, RIM - j : RIM - j + out_rows]
            for j in range(taps)
        )
    )
    key_value = filtered[1] * filtered[2]
    grad_mixed = cot_ext * filtered[0]
    kv_ext = jnp.concatenate(
        [from_behind(key_value[rows - span : rows], "seq", 1), key_value], axis=0
    )
    gm_ext = jnp.concatenate(
        [grad_mixed[:rows], from_behind(grad_mixed[: span + RIM], "seq", -1)], axis=0
    )
    fwd, inv = spectrum_tables(rows, span)
    half = fwd.shape[0] // 2
    fwd_t = jnp.asarray(fwd, BF)
    h = jnp.dot(fwd_t[:, :span], medium_taps.astype(BF), preferred_element_type=F32)
    x = jnp.dot(fwd_t, (kv_ext * 0.5).astype(BF), preferred_element_type=F32)
    g = jnp.dot(fwd_t, (gm_ext * 0.5).astype(BF), preferred_element_type=F32)
    hr, hi = (h[:half], h[half:])
    xr, xi = (x[:half], x[half:])
    gr, gi = (g[:half], g[half:])
    y = jnp.concatenate([xr * hr - xi * hi, xr * hi + xi * hr], axis=0).astype(BF)
    z = jnp.concatenate([gr * hr + gi * hi, gi * hr - gr * hi], axis=0).astype(BF)
    mixed = (
        jnp.dot(jnp.asarray(inv[span : span + out_rows], BF), y, preferred_element_type=F32)
        + skip_gain * key_value
    )
    grad_kv = (
        jnp.dot(jnp.asarray(inv[:out_rows], BF), z, preferred_element_type=F32)
        + skip_gain * gm_ext[:out_rows]
    )
    streams = jnp.stack([cot_ext * mixed, grad_kv * filtered[2], grad_kv * filtered[1]])
    grad_pre = sum(
        (short_taps[:, j][:, None, :] * streams[:, j : j + rows] for j in range(taps))
    ).astype(BF)
    wide = jnp.concatenate(
        [adapter_up_matrices, jnp.broadcast_to(sketch.T[None], (3, BUCKETS, width))], axis=1
    )
    prods = jnp.einsum("stc,skc->stk", grad_pre, wide, preferred_element_type=F32)
    sketch_in = ADAPTER_SCALE * jnp.einsum(
        "tk,str->ksr", token_sketch, prods[:, :, :rank], precision=lax.Precision.HIGHEST
    )
    sketch_out = jnp.einsum(
        "stk,tsr->ksr",
        prods[:, :, rank:],
        low[RIM : RIM + rows].reshape(rows, 3, rank).astype(F32),
        precision=lax.Precision.HIGHEST,
    )
    raw = jnp.stack([sketch_in, sketch_out]).reshape(2, BUCKETS, 3 * rank)
    raw = lax.psum(raw, ("seq", "tensor"))
    return raw * lax.rsqrt(jnp.mean(raw * raw) + FEATURE_EPS)


def solution(mesh):
    in_specs = (
        P(("parts", "seq")),
        P(None, "tensor"),
        P("tensor"),
        P(None, ("parts", "seq"), "tensor"),
        P("tensor", None),
        P(None, None, "tensor"),
        P(None, None, "tensor"),
        P(None, "tensor"),
        P("tensor"),
        P(("parts", "seq"), "tensor"),
        P("tensor"),
    )
    out_specs = P("parts", None, None)
    return jax.shard_map(
        on_device, mesh=mesh, in_specs=in_specs, out_specs=out_specs, check_vma=False
    )
```

profile of v0, /device:TPU:2, one launch (start us, length us, event | category | flops | bytes accessed | tf_op | source)
XLA Modules:
  0.0 210.0 jit_solution(11315392443431153149)
XLA Ops:
  6.5 0.8 broadcast_add_fusion
  7.4 0.1 fusion.72
  7.4 1.9 collective-permute-start
  9.4 3.6 %collective-permute-start.1 = (s32[8]{0:T(128)S(1)}, s32[8]{0:T(128)S(1)}, u32[]{:S(2)}, u32[]{:S(2)}) collective-permute-start(s32[8]{0:T(128)S(1)} %get-tuple-element.21), channel_id=1, source_target_pairs={{4,0},{8,4},{12,8},{5,1},{9,5},{13,9},{6,2},{10,6},{14,10},{7,3},{... | collective-permute-start | bytes 104 | tf_op jit(solution)/shard_map/ppermute | solution.py:19
  13.0 1.4 slice.205
  14.4 1.9 collective-permute-start.2
  16.3 1.7 slice_convert_fusion.1
  18.0 2.4 %collective-permute-start.3 = (f32[3,8,2048]{2,1,0:T(8,128)}, f32[3,8,2048]{2,1,0:T(8,128)S(1)}, u32[]{:S(2)}, u32[]{:S(2)}) collective-permute-start(f32[3,8,2048]{2,1,0:T(8,128)} %get-tuple-element.11), channel_id=1, source_target_pairs={{0,4},{4,8},{8,12},{1,5},{5,9},{9,13},{2,6},{6,10},{10,14},{3,7},{... | collective-permute-start | bytes 589832 | tf_op jit(solution)/shard_map/ppermute | solution.py:19
  20.4 3.2 %collective-permute-start.4 = (f32[3,8,2048]{2,1,0:T(8,128)}, f32[3,8,2048]{2,1,0:T(8,128)}, u32[]{:S(2)}, u32[]{:S(2)}) collective-permute-start(f32[3,8,2048]{2,1,0:T(8,128)} %get-tuple-element.12), channel_id=1, source_target_pairs={{4,0},{8,4},{12,8},{5,1},{9,5},{13,9},{6,2},{10,6},{14,10},{7,3},{... | collective-permute-start | bytes 589832 | tf_op jit(solution)/shard_map/ppermute | solution.py:19
  23.6 0.7 compare_select_fusion
  24.3 0.7 add_select_fusion
  25.0 2.7 %fusion.71 = (f32[3,1,2048]{2,1,0:T(1,128)}, f32[3,1,2048]{2,1,0:T(1,128)S(1)}, f32[3,1,2048]{2,1,0:T(1,128)S(1)}, f32[3,1,2048]{2,1,0:T(1,128)S(1)}, f32[3,1,20...) fusion(f32[3,7,2048]{2,1,0:T(8,128)} %param.20), kind=kLoop, calls=%fused_computation.129 | loop fusion | bytes 344064 | tf_op jit(solution)/shard_map/slice | solution.py:120
  27.8 0.7 select_convert_fusion
  28.6 0.1 pad_add_fusion
  28.7 0.9 multiply_reduce_fusion
  29.6 0.1 broadcast_in_dim.16
  29.7 0.0 copy-start.33
  29.7 0.0 copy-start.10
  29.7 0.8 fusion.27
  30.5 0.9 pad_maximum_fusion.3
  31.4 0.0 all-reduce.2.cloned.1.call-update
  31.5 0.7 copy_bitcast_fusion
  32.1 0.2 convert_element_type.47
  32.4 6.1 %convert_element_type.49 = f32[3,256,2048]{2,1,0:T(8,128)} convert(bf16[3,256,2048]{2,1,0:T(8,128)(2,1)} %param.17) | non-fusion elementwise | flops 1572864 | bytes 9437184 | tf_op jit(solution)/shard_map/convert_element_type | solution.py:61
  38.6 33.1 %all-reduce.2.cloned.1.call-done = f32[272,401]{1,0:T(8,128)} async-done(((f32[272,401]{1,0:T(8,128)}), f32[272,401]{1,0:T(8,128)}) %all-reduce.2.cloned.1.call-update) | async-done | bytes 436304 | tf_op jit(solution)/shard_map/psum | solution.py:78
  71.6 1.2 fusion.61
  72.9 4.4 %maximum_add_fusion = f32[3,272,2048]{2,1,0:T(8,128)S(1)} fusion(f32[3,8,2048]{2,1,0:T(8,128)} %collective-permute-done.4, f32[3,256,2048]{2,1,0:T(8,128)} %convert_element_type.49, f32[3,8,2048]{2,1,0:T(8,128)S(1)} %collective-permute-done.3, bf16[3,128,2048]{2,1,0:T(8,128)(2,1)} %param.19, f32[272]{0:T(512)S(1)} %get-tuple-element.6, ...), kind=kOutput, calls=%fused_computation | convolution fusion | flops 433041408 | bytes 15361088 | tf_op jit(solution)/shard_map/tsr,src->stc/dot_general | solution.py:82
  77.3 5.3 %fusion = f32[3,264,2048]{2,1,0:T(8,128)S(1)} fusion(f32[3,272,2048]{2,1,0:T(8,128)S(1)} %maximum_add_fusion, f32[3,2048]{1,0:T(4,128)S(1)} %copy-done.25, f32[3,2048]{1,0:T(4,128)S(1)} %copy-done.27, f32[3,2048]{1,0:T(4,128)S(1)} %get-tuple-element.26, f32[3,2048]{1,0:T(4,128)S(1)} %get-tuple-element.27, f32[3,2048]{1,0:T(4,128)S(1)} %get-tuple-element.28, ...), kind=kLoop, calls=%fused_computation.2 | loop fusion | flops 21086208 | bytes 52076544 | tf_op jit(solution)/shard_map/add | solution.py:85
  82.7 0.0 copy-start.31
  82.7 0.8 fusion.31
  83.5 1.9 copy-done.2
  85.4 1.1 slice.216
  86.5 0.6 copy-done.3
  87.2 1.9 collective-permute-start.5
  89.1 0.6 fusion.46
  89.7 1.1 slice.223
  90.8 1.6 slice.222
  92.4 0.1 slice.204
  92.4 0.1 fusion.48
  92.5 0.7 slice.236
  93.2 1.7 copy.24
  95.0 3.8 %collective-permute-start.6 = (f32[136,2048]{1,0:T(8,128)}, f32[136,2048]{1,0:T(8,128)S(1)}, u32[]{:S(2)}, u32[]{:S(2)}) collective-permute-start(f32[136,2048]{1,0:T(8,128)} %slice.223), channel_id=1, source_target_pairs={{4,0},{8,4},{12,8},{5,1},{9,5},{13,9},{6,2},{10,6},{14,10},{7,3},{... | collective-permute-start | bytes 3342344 | tf_op jit(solution)/shard_map/ppermute | solution.py:19
  98.8 0.0 copy-start.14
  98.8 4.8 %collective-permute-done.5 = f32[128,2048]{1,0:T(8,128)} collective-permute-done((f32[128,2048]{1,0:T(8,128)}, f32[128,2048]{1,0:T(8,128)}, u32[]{:S(2)}, u32[]{:S(2)}) %collective-permute-start.5) | collective-permute-done | bytes 1048608 | tf_op jit(solution)/shard_map/ppermute | solution.py:19
  103.6 3.1 %fusion.35 = f32[416,2048]{1,0:T(8,128)S(1)} fusion(bf16[416,392]{1,0:T(8,128)(2,1)} %constant.47.clone, f32[264,2048]{1,0:T(8,128)} %copy-done.3, f32[128,2048]{1,0:T(8,128)} %collective-permute-done.5), kind=kOutput, calls=%fused_computation.68 | convolution fusion | flops 670351360 | bytes 6945280 | tf_op jit(solution)/shard_map/dot_general | solution.py:103
  106.7 0.0 copy-start.15
  106.7 0.7 fusion.42
  107.4 0.9 copy-done.4
  108.3 0.6 copy-done.6
  108.9 0.9 fusion.22
  109.9 0.0 copy-start.13
  109.9 2.1 collective-permute-done.6
  111.9 1.1 fusion.37
  113.0 0.0 copy-start.16
  113.0 0.7 fusion.43
  113.7 0.2 copy-done.16
  113.9 2.8 %multiply_bitcast_fusion.1 = (f32[1,264,2048]{2,1,0:T(8,128)S(1)}, f32[1,264,2048]{2,1,0:T(8,128)S(1)}) fusion(f32[3,264,2048]{2,1,0:T(8,128)} %copy-done.2, f32[136,2048]{1,0:T(8,128)S(1)} %collective-permute-done.6, f32[256,2048]{1,0:T(8,128)S(1)} %copy-done.7, f32[2048]{0:T(1024)S(1)} %copy-done.35, f32[2048,264]{0,1:T(8,128)S(1)} %fusion.43, ...), kind=kOutput, calls=%fused_computation.55 | convolution fusion | flops 229867520 | bytes 20958464 | tf_op jit(solution)/shard_map/dot_general | solution.py:115
  116.8 3.2 %pad_maximum_fusion = f32[3,264,2048]{2,1,0:T(8,128)} fusion(f32[1,264,2048]{2,1,0:T(8,128)S(1)} %get-tuple-element.8, f32[1,264,2048]{2,1,0:T(8,128)S(1)} %get-tuple-element.7, f32[1,264,2048]{2,1,0:T(8,128)S(1)} %fusion.22), kind=kLoop, calls=%fused_computation.14 | loop fusion | flops 3244032 | bytes 12976128 | tf_op jit(solution)/shard_map/stack | solution.py:118
  120.1 18.6 %fusion.16 = f32[3,256,144]{1,2,0:T(8,128)S(1)} fusion(f32[3,264,2048]{2,1,0:T(8,128)} %pad_maximum_fusion, f32[3,2048]{1,0:T(4,128)S(1)} %copy-done.26, f32[3,2048]{1,0:T(4,128)S(1)} %copy-done.28, f32[3,2048]{1,0:T(4,128)S(1)} %copy-done.18, f32[3,2048]{1,0:T(4,128)S(1)} %copy-done.20, f32[3,2048]{1,0:T(4,128)S(1)} %copy-done.22, ...), kind=kOutput, calls=%fused_computation.36 | convolution fusion | flops 478543872 | bytes 46424064 | tf_op jit(solution)/shard_map/stc,skc->stk/dot_general | solution.py:125
  138.7 0.3 convolution_bitcast_fusion
  139.0 0.6 convolution_multiply_fusion
  139.7 61.5 %psum.15 = f32[2,16,384]{2,1,0:T(8,128)S(1)} all-reduce(f32[2,16,384]{2,1,0:T(8,128)S(1)} %pad_maximum_fusion.4), channel_id=1, replica_groups=mesh['parts'=2,'seq'=4,'tensor'=4] {'seq','tensor'}, use_global_device_ids=true, to_apply=%region_2.3 | all-reduce | flops 12288 | bytes 98304 | tf_op jit(solution)/shard_map/psum | solution.py:136
  201.2 0.6 multiply_reduce_fusion.2
  202.5 0.6 broadcast_multiply_fusion
  (83 shorter events, 0.4 us)
Async XLA Ops:
  6.5 22.1 %copy-start = (bf16[512,2048]{1,0:T(8,128)(2,1)S(1)}, bf16[512,2048]{1,0:T(8,128)(2,1)}, u32[]{:S(2)}) copy-start(bf16[512,2048]{1,0:T(8,128)(2,1)} %param.15) | copy-start | bytes 6291460
  6.5 65.1 %all-reduce.2.cloned.1.call-start = ((), (), s32[]{:S(2)}) async-start(), calls=%async_computation | async-start | bytes 1114112 | tf_op jit(solution)/shard_map/psum | solution.py:78
  7.4 21.1 %collective-permute-start = (s32[8]{0:T(128)S(1)}, s32[8]{0:T(128)S(1)}, u32[]{:S(2)}, u32[]{:S(2)}) collective-permute-start(s32[8]{0:T(128)S(1)} %get-tuple-element.20), channel_id=1, source_target_pairs={{0,4},{4,8},{8,12},{1,5},{5,9},{9,13},{2,6},{6,10},{10,14},{3,7},{... | collective-permute-start | bytes 104 | tf_op jit(solution)/shard_map/ppermute | solution.py:19
  9.4 19.2 %collective-permute-start.1 = (s32[8]{0:T(128)S(1)}, s32[8]{0:T(128)S(1)}, u32[]{:S(2)}, u32[]{:S(2)}) collective-permute-start(s32[8]{0:T(128)S(1)} %get-tuple-element.21), channel_id=1, source_target_pairs={{4,0},{8,4},{12,8},{5,1},{9,5},{13,9},{6,2},{10,6},{14,10},{7,3},{... | collective-permute-start | bytes 104 | tf_op jit(solution)/shard_map/ppermute | solution.py:19
  14.4 68.3 %collective-permute-start.2 = (f32[8,2048]{1,0:T(8,128)}, f32[8,2048]{1,0:T(8,128)S(1)}, u32[]{:S(2)}, u32[]{:S(2)}) collective-permute-start(f32[8,2048]{1,0:T(8,128)} %slice.205), channel_id=1, source_target_pairs={{4,0},{8,4},{12,8},{5,1},{9,5},{13,9},{6,2},{10,6},{14,10},{7,3},{... | collective-permute-start | bytes 196616 | tf_op jit(solution)/shard_map/ppermute | solution.py:19
  18.0 54.8 %collective-permute-start.3 = (f32[3,8,2048]{2,1,0:T(8,128)}, f32[3,8,2048]{2,1,0:T(8,128)S(1)}, u32[]{:S(2)}, u32[]{:S(2)}) collective-permute-start(f32[3,8,2048]{2,1,0:T(8,128)} %get-tuple-element.11), channel_id=1, source_target_pairs={{0,4},{4,8},{8,12},{1,5},{5,9},{9,13},{2,6},{6,10},{10,14},{3,7},{... | collective-permute-start | bytes 589832 | tf_op jit(solution)/shard_map/ppermute | solution.py:19
  20.4 52.4 %collective-permute-start.4 = (f32[3,8,2048]{2,1,0:T(8,128)}, f32[3,8,2048]{2,1,0:T(8,128)}, u32[]{:S(2)}, u32[]{:S(2)}) collective-permute-start(f32[3,8,2048]{2,1,0:T(8,128)} %get-tuple-element.12), channel_id=1, source_target_pairs={{4,0},{8,4},{12,8},{5,1},{9,5},{13,9},{6,2},{10,6},{14,10},{7,3},{... | collective-permute-start | bytes 589832 | tf_op jit(solution)/shard_map/ppermute | solution.py:19
  27.7 1.9 copy-start.36
  27.7 2.0 copy-start.37
  27.8 49.5 %copy-start.17 = (f32[3,2048]{1,0:T(4,128)}, f32[3,2048]{1,0:T(4,128)S(1)}, u32[]{:S(2)}) copy-start(f32[3,2048]{1,0:T(4,128)S(1)} %get-tuple-element.26) | copy-start | bytes 73732
  27.8 49.5 %copy-start.19 = (f32[3,2048]{1,0:T(4,128)}, f32[3,2048]{1,0:T(4,128)S(1)}, u32[]{:S(2)}) copy-start(f32[3,2048]{1,0:T(4,128)S(1)} %get-tuple-element.27) | copy-start | bytes 73732
  27.8 49.5 %copy-start.21 = (f32[3,2048]{1,0:T(4,128)}, f32[3,2048]{1,0:T(4,128)S(1)}, u32[]{:S(2)}) copy-start(f32[3,2048]{1,0:T(4,128)S(1)} %get-tuple-element.28) | copy-start | bytes 73732
  27.8 49.5 %copy-start.23 = (f32[3,2048]{1,0:T(4,128)}, f32[3,2048]{1,0:T(4,128)S(1)}, u32[]{:S(2)}) copy-start(f32[3,2048]{1,0:T(4,128)S(1)} %get-tuple-element.29) | copy-start | bytes 73732
  29.7 1.7 copy-start.33
  29.7 1.7 copy-start.34
  29.7 2.4 %copy-start.10 = (bf16[256,2048]{1,0:T(8,128)(2,1)S(1)}, bf16[256,2048]{1,0:T(8,128)(2,1)}, u32[]{:S(2)}) copy-start(bf16[256,2048]{1,0:T(8,128)(2,1)} %param.23) | copy-start | bytes 3145732
  32.4 50.4 %copy-start.5 = (f32[256,2048]{1,0:T(8,128)}, f32[256,2048]{1,0:T(8,128)S(1)}, u32[]{:S(2)}) copy-start(f32[256,2048]{1,0:T(8,128)S(1)} %convert_element_type.47) | copy-start | bytes 6291460
  32.4 6.2 %copy-start.32 = (f32[3,1,2048]{2,1,0:T(1,128)S(1)}, f32[3,1,2048]{2,1,0:T(1,128)}, u32[]{:S(2)}) copy-start(f32[3,1,2048]{2,1,0:T(1,128)} %get-tuple-element.13) | copy-start | bytes 73732
  38.5 38.7 %copy-start.29 = (f32[3,1,2048]{2,0,1:T(4,128)}, f32[3,1,2048]{2,0,1:T(4,128)S(1)}, u32[]{:S(2)}) copy-start(f32[3,1,2048]{2,0,1:T(4,128)S(1)} %copy.50) | copy-start | bytes 73732
  72.8 4.5 %copy-start.25 = (f32[3,2048]{1,0:T(4,128)S(1)}, f32[3,2048]{1,0:T(4,128)}, u32[]{:S(2)}) copy-start(f32[3,2048]{1,0:T(4,128)} %get-tuple-element.24) | copy-start | bytes 73732
  72.8 4.5 %copy-start.27 = (f32[3,2048]{1,0:T(4,128)S(1)}, f32[3,2048]{1,0:T(4,128)}, u32[]{:S(2)}) copy-start(f32[3,2048]{1,0:T(4,128)} %get-tuple-element.25) | copy-start | bytes 73732
  82.7 2.7 %copy-start.2 = (f32[3,264,2048]{2,1,0:T(8,128)}, f32[3,264,2048]{2,1,0:T(8,128)S(1)}, u32[]{:S(2)}) copy-start(f32[3,264,2048]{2,1,0:T(8,128)S(1)} %fusion) | copy-start | bytes 19464196
  82.7 6.4 %copy-start.11 = (f32[128,2048]{1,0:T(8,128)S(1)}, f32[128,2048]{1,0:T(8,128)}, u32[]{:S(2)}) copy-start(f32[128,2048]{1,0:T(8,128)} %param.21) | copy-start | bytes 3145732
  82.7 6.4 %copy-start.31 = (bf16[416,128]{1,0:T(8,128)(2,1)S(1)}, bf16[416,128]{1,0:T(8,128)(2,1)}, u32[]{:S(2)}) copy-start(bf16[416,128]{1,0:T(8,128)(2,1)} %constant.50) | copy-start | bytes 319492
  85.4 1.8 copy-start.3
  87.2 16.4 %collective-permute-start.5 = (f32[128,2048]{1,0:T(8,128)}, f32[128,2048]{1,0:T(8,128)}, u32[]{:S(2)}, u32[]{:S(2)}) collective-permute-start(f32[128,2048]{1,0:T(8,128)} %slice.216), channel_id=1, source_target_pairs={{0,4},{4,8},{8,12},{1,5},{5,9},{9,13},{2,6},{6,10},{10,14},{3,7},{... | collective-permute-start | bytes 3145736 | tf_op jit(solution)/shard_map/ppermute | solution.py:19
  89.7 2.7 %copy-start.9 = (f32[272,401]{1,0:T(8,128)S(1)}, f32[272,401]{1,0:T(8,128)}, u32[]{:S(2)}) copy-start(f32[272,401]{1,0:T(8,128)} %all-reduce.2.cloned.1.call-done) | copy-start | bytes 1308868
  95.0 17.0 %collective-permute-start.6 = (f32[136,2048]{1,0:T(8,128)}, f32[136,2048]{1,0:T(8,128)S(1)}, u32[]{:S(2)}, u32[]{:S(2)}) collective-permute-start(f32[136,2048]{1,0:T(8,128)} %slice.223), channel_id=1, source_target_pairs={{4,0},{8,4},{12,8},{5,1},{9,5},{13,9},{6,2},{10,6},{14,10},{7,3},{... | collective-permute-start | bytes 3342344 | tf_op jit(solution)/shard_map/ppermute | solution.py:19
  98.8 7.8 %copy-start.14 = (bf16[264,208]{1,0:T(8,128)(2,1)S(1)}, bf16[264,208]{1,0:T(8,128)(2,1)}, u32[]{:S(2)}) copy-start(bf16[264,208]{1,0:T(8,128)(2,1)} %constant.51) | copy-start | bytes 329476
  106.7 1.6 copy-start.4
  106.7 2.2 %copy-start.6 = (f32[256,2048]{1,0:T(8,128)S(1)}, f32[256,2048]{1,0:T(8,128)}, u32[]{:S(2)}) copy-start(f32[256,2048]{1,0:T(8,128)} %copy-done.5) | copy-start | bytes 6291460
  106.7 2.2 %copy-start.15 = (bf16[264,208]{1,0:T(8,128)(2,1)S(1)}, bf16[264,208]{1,0:T(8,128)(2,1)}, u32[]{:S(2)}) copy-start(bf16[264,208]{1,0:T(8,128)(2,1)} %constant.52) | copy-start | bytes 329476
  106.7 2.2 %copy-start.35 = (f32[2048]{0:T(1024)S(1)}, f32[2048]{0:T(1024)}, u32[]{:S(2)}) copy-start(f32[2048]{0:T(1024)} %param.22) | copy-start | bytes 24580
  108.9 3.0 %copy-start.7 = (f32[256,2048]{1,0:T(8,128)S(1)}, f32[256,2048]{1,0:T(8,128)}, u32[]{:S(2)}) copy-start(f32[256,2048]{1,0:T(8,128)} %slice.222) | copy-start | bytes 6291460
  108.9 3.0 %copy-start.8 = (bf16[416,392]{1,0:T(8,128)(2,1)S(1)}, bf16[416,392]{1,0:T(8,128)(2,1)}, u32[]{:S(2)}) copy-start(bf16[416,392]{1,0:T(8,128)(2,1)} %constant.47.clone) | copy-start | bytes 978436
  109.9 3.1 %copy-start.13 = (bf16[264,208]{1,0:T(8,128)(2,1)S(1)}, bf16[264,208]{1,0:T(8,128)(2,1)}, u32[]{:S(2)}) copy-start(bf16[264,208]{1,0:T(8,128)(2,1)} %constant.53) | copy-start | bytes 329476
  113.0 0.9 copy-start.16
  116.7 3.3 %copy-start.18 = (f32[3,2048]{1,0:T(4,128)S(1)}, f32[3,2048]{1,0:T(4,128)}, u32[]{:S(2)}) copy-start(f32[3,2048]{1,0:T(4,128)} %copy-done.17) | copy-start | bytes 73732
  116.7 3.3 %copy-start.20 = (f32[3,2048]{1,0:T(4,128)S(1)}, f32[3,2048]{1,0:T(4,128)}, u32[]{:S(2)}) copy-start(f32[3,2048]{1,0:T(4,128)} %copy-done.19) | copy-start | bytes 73732
  116.7 3.3 %copy-start.22 = (f32[3,2048]{1,0:T(4,128)S(1)}, f32[3,2048]{1,0:T(4,128)}, u32[]{:S(2)}) copy-start(f32[3,2048]{1,0:T(4,128)} %copy-done.21) | copy-start | bytes 73732
  116.7 3.3 %copy-start.24 = (f32[3,2048]{1,0:T(4,128)S(1)}, f32[3,2048]{1,0:T(4,128)}, u32[]{:S(2)}) copy-start(f32[3,2048]{1,0:T(4,128)} %copy-done.23) | copy-start | bytes 73732
  116.7 3.3 %copy-start.26 = (f32[3,2048]{1,0:T(4,128)S(1)}, f32[3,2048]{1,0:T(4,128)}, u32[]{:S(2)}) copy-start(f32[3,2048]{1,0:T(4,128)} %get-tuple-element.24) | copy-start | bytes 73732
  116.7 3.3 %copy-start.28 = (f32[3,2048]{1,0:T(4,128)S(1)}, f32[3,2048]{1,0:T(4,128)}, u32[]{:S(2)}) copy-start(f32[3,2048]{1,0:T(4,128)} %get-tuple-element.25) | copy-start | bytes 73732
  116.8 3.3 %copy-start.30 = (f32[3,1,2048]{2,0,1:T(4,128)S(1)}, f32[3,1,2048]{2,0,1:T(4,128)}, u32[]{:S(2)}) copy-start(f32[3,1,2048]{2,0,1:T(4,128)} %copy-done.29) | copy-start | bytes 73732
  120.0 18.7 %copy-start.12 = (bf16[256,384]{0,1:T(8,128)(2,1)S(1)}, bf16[256,384]{0,1:T(8,128)(2,1)}, u32[]{:S(2)}) copy-start(bf16[256,384]{0,1:T(8,128)(2,1)} %copy.24) | copy-start | bytes 589828
  120.0 18.9 %slice-start = ((f32[272,401]{1,0:T(8,128)}), f32[272,16]{1,0:T(8,128)S(1)}, s32[]{:S(2)}) async-start(f32[272,401]{1,0:T(8,128)} %all-reduce.2.cloned.1.call-done), calls=%async_computation.1 | async-start | bytes 278528 | tf_op jit(solution)/shard_map/slice | solution.py:81
  120.1 83.1 %copy-start.1 = (bf16[512,2048]{1,0:T(8,128)(2,1)S(1)}, bf16[512,2048]{1,0:T(8,128)(2,1)}, u32[]{:S(2)}) copy-start(bf16[512,2048]{1,0:T(8,128)(2,1)} %param.15) | copy-start | bytes 6291460
Sparse Core Ops, SparseCore 0:
  31.6 40.0 all-reduce.1
where the time goes:
time: 211 us; the launch traced here: 210 us
  blocking collectives  61.5 us (29%)
  waiting for transfers between devices  39.9 us (19%)
  matrix products  35.3 us (17%)
  other arithmetic  23.9 us (11%)
  starting transfers between devices  18.7 us (9%)
  local copies, waits for them, and re-layouts  15.8 us (7%)
  between operations  14.8 us (7%)
    psum x1, blocking collectives, on_device(): raw = lax.psum(raw, ('seq', 'tensor'))  61.5 us
    psum x1, waiting for transfers between devices, on_device(): total = lax.psum(jnp.concatenate([piece, squares], axis=1), 'tensor')  33.1 us
    ppermute x7, starting transfers between devices, from_behind(): return lax.ppermute(array, axis, pairs)  18.7 us
    dot_general x1, matrix products, on_device(): jnp.einsum('stc,skc->stk', grad_pre, wide, preferred_element_type=F32)  18.6 us
    ppermute x7, waiting for transfers between devices, from_behind(): return lax.ppermute(array, axis, pairs)  6.83 us
    convert_element_type x1, other arithmetic, on_device(): base_proj.astype(F32)  6.15 us
    add x1, other arithmetic, on_device(): sum((short_taps[:, j][:, None, :] * pre_mix[:, RIM - j:RIM - j + out_rows...  5.34 us
    unnamed x80, local copies, waits for them, and re-layouts  5.18 us
  transfers between devices with their start and end apart: 8, of which 3 were waited for; matrix products, arithmetic and copies ran while one was open for 19% of the time, Pallas kernels for 0%

commit v1 on v0

--- a/solution.py
+++ b/solution.py
@@ -133,7 +133,7 @@
         precision=lax.Precision.HIGHEST,
     )
     raw = jnp.stack([sketch_in, sketch_out]).reshape(2, BUCKETS, 3 * rank)
-    raw = lax.psum(raw, ("seq", "tensor"))
+    raw = lax.psum(lax.psum(raw, "tensor"), "seq")
     return raw * lax.rsqrt(jnp.mean(raw * raw) + FEATURE_EPS)
 
 

time: 211 us -> 179 us (0.85)
  blocking collectives: 61.5 us -> 29 us
    psum x1 -> x2, blocking collectives: 61.5 us -> 29 us  [on_device(): raw = lax.psum(lax.psum(raw, 'tensor'), 'seq')]
  transfers between devices with their start and end apart: 8 -> 8, of which waited for: 3 -> 3; matrix products, arithmetic and copies ran while one was open for 19% -> 22% of each run, Pallas kernels for 0% -> 0%
where the time goes in v1:
time: 179 us; the launch traced here: 178 us
  waiting for transfers between devices  39.9 us (22%)
  matrix products  35.2 us (20%)
  blocking collectives  29 us (16%)
  other arithmetic  23.9 us (13%)
  starting transfers between devices  18.7 us (10%)
  local copies, waits for them, and re-layouts  15.9 us (9%)
  between operations  14.9 us (8%)
    psum x1, waiting for transfers between devices, on_device(): total = lax.psum(jnp.concatenate([piece, squares], axis=1), 'tensor')  33.1 us
    psum x2, blocking collectives, on_device(): raw = lax.psum(lax.psum(raw, 'tensor'), 'seq')  29 us
    ppermute x7, starting transfers between devices, from_behind(): return lax.ppermute(array, axis, pairs)  18.7 us
    dot_general x1, matrix products, on_device(): jnp.einsum('stc,skc->stk', grad_pre, wide, preferred_element_type=F32)  18.6 us
    ppermute x7, waiting for transfers between devices, from_behind(): return lax.ppermute(array, axis, pairs)  6.83 us
    convert_element_type x1, other arithmetic, on_device(): base_proj.astype(F32)  6.14 us
    add x1, other arithmetic, on_device(): sum((short_taps[:, j][:, None, :] * pre_mix[:, RIM - j:RIM - j + out_rows...  5.34 us
    unnamed x80, local copies, waits for them, and re-layouts  5.26 us
  transfers between devices with their start and end apart: 8, of which 3 were waited for; matrix products, arithmetic and copies ran while one was open for 22% of the time, Pallas kernels for 0%

profile of v1, /device:TPU:2, one launch (start us, length us, event | category | flops | bytes accessed | tf_op | source)
XLA Modules:
  0.0 177.5 jit_solution(944851497084103016)
XLA Ops:
  6.5 0.8 broadcast_add_fusion
  7.4 0.1 fusion.72
  7.4 1.9 %collective-permute-start = (s32[8]{0:T(128)S(1)}, s32[8]{0:T(128)S(1)}, u32[]{:S(2)}, u32[]{:S(2)}) collective-permute-start(s32[8]{0:T(128)S(1)} %get-tuple-element.20), channel_id=1, source_target_pairs={{0,4},{4,8},{8,12},{1,5},{5,9},{9,13},{2,6},{6,10},{10,14},{3,7},{... | collective-permute-start | bytes 104 | tf_op jit(solution)/shard_map/ppermute | solution.py:19
  9.4 3.6 %collective-permute-start.1 = (s32[8]{0:T(128)S(1)}, s32[8]{0:T(128)S(1)}, u32[]{:S(2)}, u32[]{:S(2)}) collective-permute-start(s32[8]{0:T(128)S(1)} %get-tuple-element.21), channel_id=1, source_target_pairs={{4,0},{8,4},{12,8},{5,1},{9,5},{13,9},{6,2},{10,6},{14,10},{7,3},{... | collective-permute-start | bytes 104 | tf_op jit(solution)/shard_map/ppermute | solution.py:19
  13.0 1.4 slice.205
  14.4 1.9 %collective-permute-start.2 = (f32[8,2048]{1,0:T(8,128)}, f32[8,2048]{1,0:T(8,128)S(1)}, u32[]{:S(2)}, u32[]{:S(2)}) collective-permute-start(f32[8,2048]{1,0:T(8,128)} %slice.205), channel_id=1, source_target_pairs={{4,0},{8,4},{12,8},{5,1},{9,5},{13,9},{6,2},{10,6},{14,10},{7,3},{... | collective-permute-start | bytes 196616 | tf_op jit(solution)/shard_map/ppermute | solution.py:19
  16.3 1.7 slice_convert_fusion.1
  18.0 2.4 %collective-permute-start.3 = (f32[3,8,2048]{2,1,0:T(8,128)}, f32[3,8,2048]{2,1,0:T(8,128)S(1)}, u32[]{:S(2)}, u32[]{:S(2)}) collective-permute-start(f32[3,8,2048]{2,1,0:T(8,128)} %get-tuple-element.11), channel_id=1, source_target_pairs={{0,4},{4,8},{8,12},{1,5},{5,9},{9,13},{2,6},{6,10},{10,14},{3,7},{... | collective-permute-start | bytes 589832 | tf_op jit(solution)/shard_map/ppermute | solution.py:19
  20.4 3.2 %collective-permute-start.4 = (f32[3,8,2048]{2,1,0:T(8,128)}, f32[3,8,2048]{2,1,0:T(8,128)}, u32[]{:S(2)}, u32[]{:S(2)}) collective-permute-start(f32[3,8,2048]{2,1,0:T(8,128)} %get-tuple-element.12), channel_id=1, source_target_pairs={{4,0},{8,4},{12,8},{5,1},{9,5},{13,9},{6,2},{10,6},{14,10},{7,3},{... | collective-permute-start | bytes 589832 | tf_op jit(solution)/shard_map/ppermute | solution.py:19
  23.6 0.7 compare_select_fusion
  24.3 0.7 add_select_fusion
  25.0 2.7 %fusion.71 = (f32[3,1,2048]{2,1,0:T(1,128)}, f32[3,1,2048]{2,1,0:T(1,128)S(1)}, f32[3,1,2048]{2,1,0:T(1,128)S(1)}, f32[3,1,2048]{2,1,0:T(1,128)S(1)}, f32[3,1,20...) fusion(f32[3,7,2048]{2,1,0:T(8,128)} %param.20), kind=kLoop, calls=%fused_computation.129 | loop fusion | bytes 344064 | tf_op jit(solution)/shard_map/slice | solution.py:120
  27.8 0.7 select_convert_fusion
  28.6 0.1 pad_add_fusion
  28.7 0.9 multiply_reduce_fusion
  29.6 0.1 broadcast_in_dim.16
  29.7 0.0 copy-start.33
  29.7 0.8 fusion.27
  30.5 0.9 pad_maximum_fusion.3
  31.4 0.0 all-reduce.2.cloned.1.call-update
  31.5 0.6 copy_bitcast_fusion
  32.1 0.2 convert_element_type.47
  32.4 6.1 %convert_element_type.49 = f32[3,256,2048]{2,1,0:T(8,128)} convert(bf16[3,256,2048]{2,1,0:T(8,128)(2,1)} %param.17) | non-fusion elementwise | flops 1572864 | bytes 9437184 | tf_op jit(solution)/shard_map/convert_element_type | solution.py:61
  38.5 33.1 %all-reduce.2.cloned.1.call-done = f32[272,401]{1,0:T(8,128)} async-done(((f32[272,401]{1,0:T(8,128)}), f32[272,401]{1,0:T(8,128)}) %all-reduce.2.cloned.1.call-update) | async-done | bytes 436304 | tf_op jit(solution)/shard_map/psum | solution.py:78
  71.6 1.2 fusion.61
  72.8 4.4 %maximum_add_fusion = f32[3,272,2048]{2,1,0:T(8,128)S(1)} fusion(f32[3,8,2048]{2,1,0:T(8,128)} %collective-permute-done.4, f32[3,256,2048]{2,1,0:T(8,128)} %convert_element_type.49, f32[3,8,2048]{2,1,0:T(8,128)S(1)} %collective-permute-done.3, bf16[3,128,2048]{2,1,0:T(8,128)(2,1)} %param.19, f32[272]{0:T(512)S(1)} %get-tuple-element.6, ...), kind=kOutput, calls=%fused_computation | convolution fusion | flops 433041408 | bytes 15361088 | tf_op jit(solution)/shard_map/tsr,src->stc/dot_general | solution.py:82
  77.3 5.3 %fusion = f32[3,264,2048]{2,1,0:T(8,128)S(1)} fusion(f32[3,272,2048]{2,1,0:T(8,128)S(1)} %maximum_add_fusion, f32[3,2048]{1,0:T(4,128)S(1)} %copy-done.25, f32[3,2048]{1,0:T(4,128)S(1)} %copy-done.27, f32[3,2048]{1,0:T(4,128)S(1)} %get-tuple-element.26, f32[3,2048]{1,0:T(4,128)S(1)} %get-tuple-element.27, f32[3,2048]{1,0:T(4,128)S(1)} %get-tuple-element.28, ...), kind=kLoop, calls=%fused_computation.2 | loop fusion | flops 21086208 | bytes 52076544 | tf_op jit(solution)/shard_map/add | solution.py:85
  82.7 0.0 copy-start.31
  82.7 0.8 fusion.31
  83.5 2.0 %copy-done.2 = f32[3,264,2048]{2,1,0:T(8,128)} copy-done((f32[3,264,2048]{2,1,0:T(8,128)}, f32[3,264,2048]{2,1,0:T(8,128)S(1)}, u32[]{:S(2)}) %copy-start.2) | copy-done | bytes 6488088
  85.5 1.1 slice.216
  86.6 0.6 copy-done.3
  87.2 1.9 %collective-permute-start.5 = (f32[128,2048]{1,0:T(8,128)}, f32[128,2048]{1,0:T(8,128)}, u32[]{:S(2)}, u32[]{:S(2)}) collective-permute-start(f32[128,2048]{1,0:T(8,128)} %slice.216), channel_id=1, source_target_pairs={{0,4},{4,8},{8,12},{1,5},{5,9},{9,13},{2,6},{6,10},{10,14},{3,7},{... | collective-permute-start | bytes 3145736 | tf_op jit(solution)/shard_map/ppermute | solution.py:19
  89.2 0.6 fusion.46
  89.8 1.1 slice.223
  90.9 1.6 slice.222
  92.5 0.1 slice.204
  92.5 0.1 fusion.48
  92.6 0.7 slice.236
  93.3 1.7 copy.24
  95.1 3.8 %collective-permute-start.6 = (f32[136,2048]{1,0:T(8,128)}, f32[136,2048]{1,0:T(8,128)S(1)}, u32[]{:S(2)}, u32[]{:S(2)}) collective-permute-start(f32[136,2048]{1,0:T(8,128)} %slice.223), channel_id=1, source_target_pairs={{4,0},{8,4},{12,8},{5,1},{9,5},{13,9},{6,2},{10,6},{14,10},{7,3},{... | collective-permute-start | bytes 3342344 | tf_op jit(solution)/shard_map/ppermute | solution.py:19
  98.9 0.0 copy-start.14
  98.9 4.8 %collective-permute-done.5 = f32[128,2048]{1,0:T(8,128)} collective-permute-done((f32[128,2048]{1,0:T(8,128)}, f32[128,2048]{1,0:T(8,128)}, u32[]{:S(2)}, u32[]{:S(2)}) %collective-permute-start.5) | collective-permute-done | bytes 1048608 | tf_op jit(solution)/shard_map/ppermute | solution.py:19
  103.7 3.1 %fusion.35 = f32[416,2048]{1,0:T(8,128)S(1)} fusion(bf16[416,392]{1,0:T(8,128)(2,1)} %constant.47.clone, f32[264,2048]{1,0:T(8,128)} %copy-done.3, f32[128,2048]{1,0:T(8,128)} %collective-permute-done.5), kind=kOutput, calls=%fused_computation.68 | convolution fusion | flops 670351360 | bytes 6945280 | tf_op jit(solution)/shard_map/dot_general | solution.py:103
  106.8 0.0 copy-start.15
  106.8 0.7 fusion.42
  107.4 0.9 copy-done.4
  108.4 0.6 copy-done.6
  109.0 0.9 fusion.22
  110.0 0.0 copy-start.13
  110.0 2.1 %collective-permute-done.6 = f32[136,2048]{1,0:T(8,128)S(1)} collective-permute-done((f32[136,2048]{1,0:T(8,128)}, f32[136,2048]{1,0:T(8,128)S(1)}, u32[]{:S(2)}, u32[]{:S(2)}) %collective-permute-start.6) | collective-permute-done | bytes 1114144 | tf_op jit(solution)/shard_map/ppermute | solution.py:19
  112.0 1.1 fusion.37
  113.1 0.0 copy-start.16
  113.1 0.7 fusion.43
  113.8 0.2 copy-done.16
  114.0 2.8 %multiply_bitcast_fusion.1 = (f32[1,264,2048]{2,1,0:T(8,128)S(1)}, f32[1,264,2048]{2,1,0:T(8,128)S(1)}) fusion(f32[3,264,2048]{2,1,0:T(8,128)} %copy-done.2, f32[136,2048]{1,0:T(8,128)S(1)} %collective-permute-done.6, f32[256,2048]{1,0:T(8,128)S(1)} %copy-done.7, f32[2048]{0:T(1024)S(1)} %copy-done.35, f32[2048,264]{0,1:T(8,128)S(1)} %fusion.43, ...), kind=kOutput, calls=%fused_computation.55 | convolution fusion | flops 229867520 | bytes 20958464 | tf_op jit(solution)/shard_map/dot_general | solution.py:115
  116.8 3.2 %pad_maximum_fusion = f32[3,264,2048]{2,1,0:T(8,128)} fusion(f32[1,264,2048]{2,1,0:T(8,128)S(1)} %get-tuple-element.8, f32[1,264,2048]{2,1,0:T(8,128)S(1)} %get-tuple-element.7, f32[1,264,2048]{2,1,0:T(8,128)S(1)} %fusion.22), kind=kLoop, calls=%fused_computation.14 | loop fusion | flops 3244032 | bytes 12976128 | tf_op jit(solution)/shard_map/stack | solution.py:118
  120.1 18.6 %fusion.16 = f32[3,256,144]{1,2,0:T(8,128)S(1)} fusion(f32[3,264,2048]{2,1,0:T(8,128)} %pad_maximum_fusion, f32[3,2048]{1,0:T(4,128)S(1)} %copy-done.26, f32[3,2048]{1,0:T(4,128)S(1)} %copy-done.28, f32[3,2048]{1,0:T(4,128)S(1)} %copy-done.18, f32[3,2048]{1,0:T(4,128)S(1)} %copy-done.20, f32[3,2048]{1,0:T(4,128)S(1)} %copy-done.22, ...), kind=kOutput, calls=%fused_computation.36 | convolution fusion | flops 478543872 | bytes 46424064 | tf_op jit(solution)/shard_map/stc,skc->stk/dot_general | solution.py:125
  138.7 0.3 convolution_bitcast_fusion
  139.0 0.6 convolution_multiply_fusion
  139.7 18.4 %psum.22 = f32[2,16,384]{2,1,0:T(8,128)S(1)} all-reduce(f32[2,16,384]{2,1,0:T(8,128)S(1)} %pad_maximum_fusion.4), channel_id=1, replica_groups=mesh['parts'=2,'seq'=4,'tensor'=4] {'tensor'}, use_global_device_ids=true, to_apply=%region_2.3 | all-reduce | flops 12288 | bytes 98304 | tf_op jit(solution)/shard_map/psum | solution.py:136
  158.2 10.6 %psum.23 = f32[2,16,384]{2,1,0:T(8,128)S(1)} all-reduce(f32[2,16,384]{2,1,0:T(8,128)S(1)} %psum.22), channel_id=1, replica_groups=mesh['parts'=2,'seq'=4,'tensor'=4] {'seq'}, use_global_device_ids=true, to_apply=%region_3.4 | all-reduce | flops 12288 | bytes 98304 | tf_op jit(solution)/shard_map/psum | solution.py:136
  168.7 0.6 multiply_reduce_fusion.2
  170.0 0.6 broadcast_multiply_fusion
  (84 shorter events, 0.4 us)
Async XLA Ops:
  6.5 22.1 %copy-start = (bf16[512,2048]{1,0:T(8,128)(2,1)S(1)}, bf16[512,2048]{1,0:T(8,128)(2,1)}, u32[]{:S(2)}) copy-start(bf16[512,2048]{1,0:T(8,128)(2,1)} %param.15) | copy-start | bytes 6291460
  6.5 65.1 %all-reduce.2.cloned.1.call-start = ((), (), s32[]{:S(2)}) async-start(), calls=%async_computation | async-start | bytes 1114112 | tf_op jit(solution)/shard_map/psum | solution.py:78
  7.4 21.1 %collective-permute-start = (s32[8]{0:T(128)S(1)}, s32[8]{0:T(128)S(1)}, u32[]{:S(2)}, u32[]{:S(2)}) collective-permute-start(s32[8]{0:T(128)S(1)} %get-tuple-element.20), channel_id=1, source_target_pairs={{0,4},{4,8},{8,12},{1,5},{5,9},{9,13},{2,6},{6,10},{10,14},{3,7},{... | collective-permute-start | bytes 104 | tf_op jit(solution)/shard_map/ppermute | solution.py:19
  9.4 19.2 %collective-permute-start.1 = (s32[8]{0:T(128)S(1)}, s32[8]{0:T(128)S(1)}, u32[]{:S(2)}, u32[]{:S(2)}) collective-permute-start(s32[8]{0:T(128)S(1)} %get-tuple-element.21), channel_id=1, source_target_pairs={{4,0},{8,4},{12,8},{5,1},{9,5},{13,9},{6,2},{10,6},{14,10},{7,3},{... | collective-permute-start | bytes 104 | tf_op jit(solution)/shard_map/ppermute | solution.py:19
  14.4 68.3 %collective-permute-start.2 = (f32[8,2048]{1,0:T(8,128)}, f32[8,2048]{1,0:T(8,128)S(1)}, u32[]{:S(2)}, u32[]{:S(2)}) collective-permute-start(f32[8,2048]{1,0:T(8,128)} %slice.205), channel_id=1, source_target_pairs={{4,0},{8,4},{12,8},{5,1},{9,5},{13,9},{6,2},{10,6},{14,10},{7,3},{... | collective-permute-start | bytes 196616 | tf_op jit(solution)/shard_map/ppermute | solution.py:19
  18.0 54.8 %collective-permute-start.3 = (f32[3,8,2048]{2,1,0:T(8,128)}, f32[3,8,2048]{2,1,0:T(8,128)S(1)}, u32[]{:S(2)}, u32[]{:S(2)}) collective-permute-start(f32[3,8,2048]{2,1,0:T(8,128)} %get-tuple-element.11), channel_id=1, source_target_pairs={{0,4},{4,8},{8,12},{1,5},{5,9},{9,13},{2,6},{6,10},{10,14},{3,7},{... | collective-permute-start | bytes 589832 | tf_op jit(solution)/shard_map/ppermute | solution.py:19
  20.4 52.4 %collective-permute-start.4 = (f32[3,8,2048]{2,1,0:T(8,128)}, f32[3,8,2048]{2,1,0:T(8,128)}, u32[]{:S(2)}, u32[]{:S(2)}) collective-permute-start(f32[3,8,2048]{2,1,0:T(8,128)} %get-tuple-element.12), channel_id=1, source_target_pairs={{4,0},{8,4},{12,8},{5,1},{9,5},{13,9},{6,2},{10,6},{14,10},{7,3},{... | collective-permute-start | bytes 589832 | tf_op jit(solution)/shard_map/ppermute | solution.py:19
  27.7 1.9 %copy-start.36 = (bf16[2048,384]{1,0:T(8,128)(2,1)S(1)}, bf16[2048,384]{1,0:T(8,128)(2,1)}, u32[]{:S(2)}) copy-start(bf16[2048,384]{1,0:T(8,128)(2,1)} %param.18) | copy-start | bytes 4718596
  27.7 2.0 %copy-start.37 = (f32[2048]{0:T(1024)S(1)}, f32[2048]{0:T(1024)}, u32[]{:S(2)}) copy-start(f32[2048]{0:T(1024)} %param.16) | copy-start | bytes 24580
  27.8 49.5 %copy-start.17 = (f32[3,2048]{1,0:T(4,128)}, f32[3,2048]{1,0:T(4,128)S(1)}, u32[]{:S(2)}) copy-start(f32[3,2048]{1,0:T(4,128)S(1)} %get-tuple-element.26) | copy-start | bytes 73732
  27.8 49.5 %copy-start.19 = (f32[3,2048]{1,0:T(4,128)}, f32[3,2048]{1,0:T(4,128)S(1)}, u32[]{:S(2)}) copy-start(f32[3,2048]{1,0:T(4,128)S(1)} %get-tuple-element.27) | copy-start | bytes 73732
  27.8 49.4 %copy-start.21 = (f32[3,2048]{1,0:T(4,128)}, f32[3,2048]{1,0:T(4,128)S(1)}, u32[]{:S(2)}) copy-start(f32[3,2048]{1,0:T(4,128)S(1)} %get-tuple-element.28) | copy-start | bytes 73732
  27.8 49.4 %copy-start.23 = (f32[3,2048]{1,0:T(4,128)}, f32[3,2048]{1,0:T(4,128)S(1)}, u32[]{:S(2)}) copy-start(f32[3,2048]{1,0:T(4,128)S(1)} %get-tuple-element.29) | copy-start | bytes 73732
  29.7 1.8 copy-start.33
  29.7 1.8 copy-start.34
  29.7 2.4 %copy-start.10 = (bf16[256,2048]{1,0:T(8,128)(2,1)S(1)}, bf16[256,2048]{1,0:T(8,128)(2,1)}, u32[]{:S(2)}) copy-start(bf16[256,2048]{1,0:T(8,128)(2,1)} %param.23) | copy-start | bytes 3145732
  32.4 50.3 %copy-start.5 = (f32[256,2048]{1,0:T(8,128)}, f32[256,2048]{1,0:T(8,128)S(1)}, u32[]{:S(2)}) copy-start(f32[256,2048]{1,0:T(8,128)S(1)} %convert_element_type.47) | copy-start | bytes 6291460
  32.4 6.2 %copy-start.32 = (f32[3,1,2048]{2,1,0:T(1,128)S(1)}, f32[3,1,2048]{2,1,0:T(1,128)}, u32[]{:S(2)}) copy-start(f32[3,1,2048]{2,1,0:T(1,128)} %get-tuple-element.13) | copy-start | bytes 73732
  38.5 38.7 %copy-start.29 = (f32[3,1,2048]{2,0,1:T(4,128)}, f32[3,1,2048]{2,0,1:T(4,128)S(1)}, u32[]{:S(2)}) copy-start(f32[3,1,2048]{2,0,1:T(4,128)S(1)} %copy.50) | copy-start | bytes 73732
  72.8 4.5 %copy-start.25 = (f32[3,2048]{1,0:T(4,128)S(1)}, f32[3,2048]{1,0:T(4,128)}, u32[]{:S(2)}) copy-start(f32[3,2048]{1,0:T(4,128)} %get-tuple-element.24) | copy-start | bytes 73732
  72.8 4.5 %copy-start.27 = (f32[3,2048]{1,0:T(4,128)S(1)}, f32[3,2048]{1,0:T(4,128)}, u32[]{:S(2)}) copy-start(f32[3,2048]{1,0:T(4,128)} %get-tuple-element.25) | copy-start | bytes 73732
  82.6 2.8 %copy-start.2 = (f32[3,264,2048]{2,1,0:T(8,128)}, f32[3,264,2048]{2,1,0:T(8,128)S(1)}, u32[]{:S(2)}) copy-start(f32[3,264,2048]{2,1,0:T(8,128)S(1)} %fusion) | copy-start | bytes 19464196
  82.7 6.5 %copy-start.11 = (f32[128,2048]{1,0:T(8,128)S(1)}, f32[128,2048]{1,0:T(8,128)}, u32[]{:S(2)}) copy-start(f32[128,2048]{1,0:T(8,128)} %param.21) | copy-start | bytes 3145732
  82.7 6.5 %copy-start.31 = (bf16[416,128]{1,0:T(8,128)(2,1)S(1)}, bf16[416,128]{1,0:T(8,128)(2,1)}, u32[]{:S(2)}) copy-start(bf16[416,128]{1,0:T(8,128)(2,1)} %constant.50) | copy-start | bytes 319492
  85.5 1.8 copy-start.3
  87.2 16.4 %collective-permute-start.5 = (f32[128,2048]{1,0:T(8,128)}, f32[128,2048]{1,0:T(8,128)}, u32[]{:S(2)}, u32[]{:S(2)}) collective-permute-start(f32[128,2048]{1,0:T(8,128)} %slice.216), channel_id=1, source_target_pairs={{0,4},{4,8},{8,12},{1,5},{5,9},{9,13},{2,6},{6,10},{10,14},{3,7},{... | collective-permute-start | bytes 3145736 | tf_op jit(solution)/shard_map/ppermute | solution.py:19
  89.8 2.7 %copy-start.9 = (f32[272,401]{1,0:T(8,128)S(1)}, f32[272,401]{1,0:T(8,128)}, u32[]{:S(2)}) copy-start(f32[272,401]{1,0:T(8,128)} %all-reduce.2.cloned.1.call-done) | copy-start | bytes 1308868
  95.1 16.9 %collective-permute-start.6 = (f32[136,2048]{1,0:T(8,128)}, f32[136,2048]{1,0:T(8,128)S(1)}, u32[]{:S(2)}, u32[]{:S(2)}) collective-permute-start(f32[136,2048]{1,0:T(8,128)} %slice.223), channel_id=1, source_target_pairs={{4,0},{8,4},{12,8},{5,1},{9,5},{13,9},{6,2},{10,6},{14,10},{7,3},{... | collective-permute-start | bytes 3342344 | tf_op jit(solution)/shard_map/ppermute | solution.py:19
  98.9 7.8 %copy-start.14 = (bf16[264,208]{1,0:T(8,128)(2,1)S(1)}, bf16[264,208]{1,0:T(8,128)(2,1)}, u32[]{:S(2)}) copy-start(bf16[264,208]{1,0:T(8,128)(2,1)} %constant.51) | copy-start | bytes 329476
  106.7 1.6 copy-start.4
  106.8 2.2 %copy-start.6 = (f32[256,2048]{1,0:T(8,128)S(1)}, f32[256,2048]{1,0:T(8,128)}, u32[]{:S(2)}) copy-start(f32[256,2048]{1,0:T(8,128)} %copy-done.5) | copy-start | bytes 6291460
  106.8 2.2 %copy-start.15 = (bf16[264,208]{1,0:T(8,128)(2,1)S(1)}, bf16[264,208]{1,0:T(8,128)(2,1)}, u32[]{:S(2)}) copy-start(bf16[264,208]{1,0:T(8,128)(2,1)} %constant.52) | copy-start | bytes 329476
  106.8 2.2 %copy-start.35 = (f32[2048]{0:T(1024)S(1)}, f32[2048]{0:T(1024)}, u32[]{:S(2)}) copy-start(f32[2048]{0:T(1024)} %param.22) | copy-start | bytes 24580
  109.0 3.0 %copy-start.7 = (f32[256,2048]{1,0:T(8,128)S(1)}, f32[256,2048]{1,0:T(8,128)}, u32[]{:S(2)}) copy-start(f32[256,2048]{1,0:T(8,128)} %slice.222) | copy-start | bytes 6291460
  109.0 3.0 %copy-start.8 = (bf16[416,392]{1,0:T(8,128)(2,1)S(1)}, bf16[416,392]{1,0:T(8,128)(2,1)}, u32[]{:S(2)}) copy-start(bf16[416,392]{1,0:T(8,128)(2,1)} %constant.47.clone) | copy-start | bytes 978436
  110.0 3.1 %copy-start.13 = (bf16[264,208]{1,0:T(8,128)(2,1)S(1)}, bf16[264,208]{1,0:T(8,128)(2,1)}, u32[]{:S(2)}) copy-start(bf16[264,208]{1,0:T(8,128)(2,1)} %constant.53) | copy-start | bytes 329476
  113.1 0.9 copy-start.16
  116.8 3.3 %copy-start.18 = (f32[3,2048]{1,0:T(4,128)S(1)}, f32[3,2048]{1,0:T(4,128)}, u32[]{:S(2)}) copy-start(f32[3,2048]{1,0:T(4,128)} %copy-done.17) | copy-start | bytes 73732
  116.8 3.3 %copy-start.20 = (f32[3,2048]{1,0:T(4,128)S(1)}, f32[3,2048]{1,0:T(4,128)}, u32[]{:S(2)}) copy-start(f32[3,2048]{1,0:T(4,128)} %copy-done.19) | copy-start | bytes 73732
  116.8 3.3 %copy-start.22 = (f32[3,2048]{1,0:T(4,128)S(1)}, f32[3,2048]{1,0:T(4,128)}, u32[]{:S(2)}) copy-start(f32[3,2048]{1,0:T(4,128)} %copy-done.21) | copy-start | bytes 73732
  116.8 3.3 %copy-start.24 = (f32[3,2048]{1,0:T(4,128)S(1)}, f32[3,2048]{1,0:T(4,128)}, u32[]{:S(2)}) copy-start(f32[3,2048]{1,0:T(4,128)} %copy-done.23) | copy-start | bytes 73732
  116.8 3.3 %copy-start.26 = (f32[3,2048]{1,0:T(4,128)S(1)}, f32[3,2048]{1,0:T(4,128)}, u32[]{:S(2)}) copy-start(f32[3,2048]{1,0:T(4,128)} %get-tuple-element.24) | copy-start | bytes 73732
  116.8 3.3 %copy-start.28 = (f32[3,2048]{1,0:T(4,128)S(1)}, f32[3,2048]{1,0:T(4,128)}, u32[]{:S(2)}) copy-start(f32[3,2048]{1,0:T(4,128)} %get-tuple-element.25) | copy-start | bytes 73732
  116.8 3.3 %copy-start.30 = (f32[3,1,2048]{2,0,1:T(4,128)S(1)}, f32[3,1,2048]{2,0,1:T(4,128)}, u32[]{:S(2)}) copy-start(f32[3,1,2048]{2,0,1:T(4,128)} %copy-done.29) | copy-start | bytes 73732
  120.1 18.6 %copy-start.12 = (bf16[256,384]{0,1:T(8,128)(2,1)S(1)}, bf16[256,384]{0,1:T(8,128)(2,1)}, u32[]{:S(2)}) copy-start(bf16[256,384]{0,1:T(8,128)(2,1)} %copy.24) | copy-start | bytes 589828
  120.1 18.9 %slice-start = ((f32[272,401]{1,0:T(8,128)}), f32[272,16]{1,0:T(8,128)S(1)}, s32[]{:S(2)}) async-start(f32[272,401]{1,0:T(8,128)} %all-reduce.2.cloned.1.call-done), calls=%async_computation.1 | async-start | bytes 278528 | tf_op jit(solution)/shard_map/slice | solution.py:81
  120.1 50.5 %copy-start.1 = (bf16[512,2048]{1,0:T(8,128)(2,1)S(1)}, bf16[512,2048]{1,0:T(8,128)(2,1)}, u32[]{:S(2)}) copy-start(bf16[512,2048]{1,0:T(8,128)(2,1)} %param.15) | copy-start | bytes 6291460
Sparse Core Ops, SparseCore 0:
  31.6 40.0 all-reduce.1
